TPU v7x, 32 devices: a whole 2x2x4 slice. The times are simulated.
32 devices in a mesh: dp: 8 (over z, x), fsdp: 4 (over y, core).
Axes of the slice: x: 2, y: 2, z: 4, core: 2. Of those that a mesh axis runs over, the one named last changes fastest.
Arguments:
- tokens: bfloat16 [640, 197, 384], P(('dp', 'fsdp')), may hold values from -6 to 6
- image_count: int32 [32], P(('dp', 'fsdp')), may hold values from 1 to 20, as said below
- w_qkv: bfloat16 [442368], P(('dp', 'fsdp')), may hold values from -0.3125 to 0.3125
- w_out: bfloat16 [147456], P(('dp', 'fsdp')), may hold values from -1.25 to 1.25
- w_fc1: bfloat16 [589824], P(('dp', 'fsdp')), may hold values from -0.3125 to 0.3125
- w_fc2: bfloat16 [589824], P(('dp', 'fsdp')), may hold values from -0.15625 to 0.15625
- norm_bias: bfloat16 [4608], P(('dp', 'fsdp')), may hold values from -1.5 to 1.5, as said below
- cotangent: bfloat16 [640, 197, 384], P(('dp', 'fsdp')), may hold values from -6 to 6
Outputs:
- output: bfloat16 [640, 197, 384], P(('dp', 'fsdp'))
- grad_tokens: bfloat16 [640, 197, 384], P(('dp', 'fsdp'))
- grad_qkv: float32 [442368], P(('dp', 'fsdp'))
- grad_out: float32 [147456], P(('dp', 'fsdp'))
- grad_fc1: float32 [589824], P(('dp', 'fsdp'))
- grad_fc2: float32 [589824], P(('dp', 'fsdp'))
- grad_norm_bias: float32 [4608], P(('dp', 'fsdp'))
Inputs may be any that keep to these rules, and one draw needn't show every extreme that they name: `image_count`: live images among a device's 20 slots, the first ones; some device holds 20. `norm_bias`: gains near one, biases and shifts of either sign.
All inputs are finite; a program needn't handle non-finite values.
Results may differ from a plain program's by a relative error of at most 0.011.
Values may be sent and summed in bfloat16 or wider, within the bound.
A program may use at most 256 MiB of HBM per device.

v0:
```python
import math

import jax
import jax.numpy as jnp
from jax import lax
from jax.sharding import PartitionSpec as P

HEADS = 6
HEAD_DIM = 64


epsilon = 1e-06


def norm_parts(values):
    center = values - jnp.mean(values, axis=-1, keepdims=True)
    inverse = lax.rsqrt(jnp.mean(center * center, axis=-1, keepdims=True) + epsilon)
    return (center * inverse, inverse)


def norm_back(upstream, normed, inverse, gain):
    scaled = upstream * gain
    return inverse * (
        scaled
        - jnp.mean(scaled, axis=-1, keepdims=True)
        - normed * jnp.mean(scaled * normed, axis=-1, keepdims=True)
    )


def gelu_slope(inputs):
    cumul = 0.5 * (1.0 + jax.scipy.special.erf(inputs * 0.7071067811865476))
    density = jnp.exp(-0.5 * inputs * inputs) * 0.3989422804014327
    return cumul + inputs * density


def over_rows(left, right):
    return lax.dot_general(
        left, right, (((0,), (0,)), ((), ())), preferred_element_type=jnp.float32
    )


def times_trans(left, right):
    return lax.dot_general(
        left, right, (((1,), (1,)), ((), ())), preferred_element_type=jnp.float32
    )


def unpack(whole, width):
    wqkv, wout, wup, wdown, small = whole
    hidden_units = wup.shape[0] // width
    cuts = [width * step for step in range(1, 8)] + [7 * width + hidden_units]
    pieces = jnp.split(small.astype(jnp.float32), cuts)
    mats = (
        wqkv.reshape(width, 3 * width),
        wout.reshape(width, width),
        wup.reshape(width, hidden_units),
        wdown.reshape(hidden_units, width),
    )
    return (mats, pieces)


def body(tokens, image_count, w_qkv, w_out, w_fc1, w_fc2, norm_bias, cotangent):
    slots, seq_len, width = tokens.shape
    rows = slots * seq_len
    scale = 1.0 / math.sqrt(HEAD_DIM)
    shards = (w_qkv, w_out, w_fc1, w_fc2, norm_bias)
    gathered = (
        lax.all_gather(shards[0], ("dp", "fsdp"), axis=0, tiled=True),
        lax.all_gather(shards[1], ("dp", "fsdp"), axis=0, tiled=True),
        lax.all_gather(shards[2], ("dp", "fsdp"), axis=0, tiled=True),
        lax.all_gather(shards[3], ("dp", "fsdp"), axis=0, tiled=True),
        lax.all_gather(shards[4], ("dp", "fsdp"), axis=0, tiled=True),
    )
    mats, pieces = unpack(gathered, width)
    wqkv, wout, wup, wdown = mats
    gain_one, shift_one, bias_q, bias_v, bias_o, gain_two, shift_two, bias_up, bias_down = pieces
    inputs = tokens.astype(jnp.float32).reshape(rows, width)
    normed_one, inverse_one = norm_parts(inputs)
    first_in = (normed_one * gain_one + shift_one).astype(jnp.bfloat16)
    project = jnp.dot(first_in, wqkv, preferred_element_type=jnp.float32)
    queries = (project[:, :width] + bias_q).astype(jnp.bfloat16)
    key_part = project[:, width : 2 * width].astype(jnp.bfloat16)
    value_part = (project[:, 2 * width :] + bias_v).astype(jnp.bfloat16)
    query_heads = queries.reshape(slots, seq_len, HEADS, HEAD_DIM)
    key_heads = key_part.reshape(slots, seq_len, HEADS, HEAD_DIM)
    value_heads = value_part.reshape(slots, seq_len, HEADS, HEAD_DIM)
    scores = (
        jnp.einsum("ishd,ithd->ihst", query_heads, key_heads, preferred_element_type=jnp.float32)
        * scale
    )
    maximum = jnp.max(scores, axis=-1, keepdims=True)
    expo = jnp.exp(scores - maximum)
    totals = jnp.sum(expo, axis=-1, keepdims=True)
    log_total = maximum + jnp.log(totals)
    attend = (expo / totals).astype(jnp.bfloat16)
    mixed = jnp.einsum("ihst,ithd->ishd", attend, value_heads, preferred_element_type=jnp.float32)
    mixed = mixed.reshape(rows, width).astype(jnp.bfloat16)
    middle = inputs + jnp.dot(mixed, wout, preferred_element_type=jnp.float32) + bias_o
    normed_two, inverse_two = norm_parts(middle)
    second_in = (normed_two * gain_two + shift_two).astype(jnp.bfloat16)
    hidden = jnp.dot(second_in, wup, preferred_element_type=jnp.float32) + bias_up
    active = jax.nn.gelu(hidden, approximate=False).astype(jnp.bfloat16)
    result = middle + jnp.dot(active, wdown, preferred_element_type=jnp.float32) + bias_down
    alive = (jnp.arange(slots) < image_count[0]).astype(jnp.float32)[:, None, None]
    output = (result.reshape(slots, seq_len, width) * alive).astype(jnp.bfloat16)
    again = (
        lax.all_gather(shards[0], ("dp", "fsdp"), axis=0, tiled=True),
        lax.all_gather(shards[1], ("dp", "fsdp"), axis=0, tiled=True),
        lax.all_gather(shards[2], ("dp", "fsdp"), axis=0, tiled=True),
        lax.all_gather(shards[3], ("dp", "fsdp"), axis=0, tiled=True),
        lax.all_gather(shards[4], ("dp", "fsdp"), axis=0, tiled=True),
    )
    back_mats, back_pieces = unpack(again, width)
    wqkv_b, wout_b, wup_b, wdown_b = back_mats
    gain_one_b = back_pieces[0]
    gain_two_b = back_pieces[5]
    upstream = (cotangent.astype(jnp.float32) * alive).reshape(rows, width)
    down_grad = upstream.astype(jnp.bfloat16)
    grad_bias_down = jnp.sum(down_grad.astype(jnp.float32), axis=0)
    grad_down = over_rows(active, down_grad)
    active_grad = times_trans(down_grad, wdown_b)
    hidden_grad = (active_grad * gelu_slope(hidden)).astype(jnp.bfloat16)
    grad_bias_up = jnp.sum(hidden_grad.astype(jnp.float32), axis=0)
    grad_up = over_rows(second_in, hidden_grad)
    second_grad = times_trans(hidden_grad, wup_b)
    grad_gain_two = jnp.sum(second_grad * normed_two, axis=0)
    grad_shift_two = jnp.sum(second_grad, axis=0)
    middle_grad = upstream + norm_back(second_grad, normed_two, inverse_two, gain_two_b)
    branch_grad = middle_grad.astype(jnp.bfloat16)
    grad_bias_o = jnp.sum(branch_grad.astype(jnp.float32), axis=0)
    grad_wout = over_rows(mixed, branch_grad)
    mixed_grad = times_trans(branch_grad, wout_b).astype(jnp.bfloat16)
    mixed_heads = mixed_grad.reshape(slots, seq_len, HEADS, HEAD_DIM)
    again_scores = (
        jnp.einsum("ishd,ithd->ihst", query_heads, key_heads, preferred_element_type=jnp.float32)
        * scale
    )
    recalled = jnp.exp(again_scores - log_total)
    attend_grad = jnp.einsum(
        "ishd,ithd->ihst", mixed_heads, value_heads, preferred_element_type=jnp.float32
    )
    value_grad = jnp.einsum(
        "ihst,ishd->ithd",
        recalled.astype(jnp.bfloat16),
        mixed_heads,
        preferred_element_type=jnp.float32,
    ).astype(jnp.bfloat16)
    inner = jnp.sum(recalled * attend_grad, axis=-1, keepdims=True)
    score_grad = (recalled * (attend_grad - inner)).astype(jnp.bfloat16)
    query_grad = (
        jnp.einsum("ihst,ithd->ishd", score_grad, key_heads, preferred_element_type=jnp.float32)
        * scale
    ).astype(jnp.bfloat16)
    key_grad = (
        jnp.einsum("ihst,ishd->ithd", score_grad, query_heads, preferred_element_type=jnp.float32)
        * scale
    ).astype(jnp.bfloat16)
    project_grad = jnp.concatenate(
        [
            query_grad.reshape(rows, width),
            key_grad.reshape(rows, width),
            value_grad.reshape(rows, width),
        ],
        axis=1,
    )
    grad_bias_q = jnp.sum(query_grad.reshape(rows, width).astype(jnp.float32), axis=0)
    grad_bias_v = jnp.sum(value_grad.reshape(rows, width).astype(jnp.float32), axis=0)
    grad_wqkv = over_rows(first_in, project_grad)
    first_grad = times_trans(project_grad, wqkv_b)
    grad_gain_one = jnp.sum(first_grad * normed_one, axis=0)
    grad_shift_one = jnp.sum(first_grad, axis=0)
    input_grad = middle_grad + norm_back(first_grad, normed_one, inverse_one, gain_one_b)
    grad_tokens = input_grad.reshape(slots, seq_len, width).astype(jnp.bfloat16)
    small_grad = jnp.concatenate(
        [
            grad_gain_one,
            grad_shift_one,
            grad_bias_q,
            grad_bias_v,
            grad_bias_o,
            grad_gain_two,
            grad_shift_two,
            grad_bias_up,
            grad_bias_down,
        ]
    )
    terms = (
        grad_wqkv.reshape(-1),
        grad_wout.reshape(-1),
        grad_up.reshape(-1),
        grad_down.reshape(-1),
        small_grad,
    )
    summed = (
        lax.psum_scatter(terms[0], ("dp", "fsdp"), scatter_dimension=0, tiled=True),
        lax.psum_scatter(terms[1], ("dp", "fsdp"), scatter_dimension=0, tiled=True),
        lax.psum_scatter(terms[2], ("dp", "fsdp"), scatter_dimension=0, tiled=True),
        lax.psum_scatter(terms[3], ("dp", "fsdp"), scatter_dimension=0, tiled=True),
        lax.psum_scatter(terms[4], ("dp", "fsdp"), scatter_dimension=0, tiled=True),
    )
    return (output, grad_tokens, summed[0], summed[1], summed[2], summed[3], summed[4])


def solution(mesh):
    return jax.shard_map(
        body,
        mesh=mesh,
        in_specs=(
            P(("dp", "fsdp"), None, None),
            P(("dp", "fsdp")),
            P(("dp", "fsdp")),
            P(("dp", "fsdp")),
            P(("dp", "fsdp")),
            P(("dp", "fsdp")),
            P(("dp", "fsdp")),
            P(("dp", "fsdp"), None, None),
        ),
        out_specs=(
            P(("dp", "fsdp"), None, None),
            P(("dp", "fsdp"), None, None),
            P(("dp", "fsdp")),
            P(("dp", "fsdp")),
            P(("dp", "fsdp")),
            P(("dp", "fsdp")),
            P(("dp", "fsdp")),
        ),
        check_vma=False,
    )
```

profile of v0, /device:TPU:11, one launch (start us, length us, event | category | flops | bytes accessed | tf_op | source)
XLA Modules:
  0.0 817.3 jit_solution(7804196128942783375)
XLA Ops:
  9.6 39.7 %all-reduce = bf16[4608]{0:T(1024)(128)(2,1)S(1)} all-reduce(bf16[4608]{0:T(1024)(128)(2,1)S(1)} %dynamic-update-slice), channel_id=1, replica_groups=mesh['dp'=8,'fsdp'=4] {'dp','fsdp'}, use_global_device_ids=true, to_apply=%add | all-reduce | flops 4608 | bytes 18432
  61.6 36.1 %all-gather.1 = bf16[32,1,4608]{2,1,0:T(2,128)(2,1)} all-gather(bf16[1,1,4608]{2,1,0:T(2,128)(2,1)S(1)} %reshape.210), channel_id=1, replica_groups=mesh['dp'=8,'fsdp'=4] {'dp','fsdp'}, dimensions={0}, use_global_device_ids=true | all-gather | bytes 304128 | tf_op jit(solution)/shard_map/all_gather | solution.py:69
  102.4 45.4 %all-gather = bf16[32,1,13824]{2,1,0:T(2,128)(2,1)} all-gather(bf16[1,1,13824]{2,1,0:T(2,128)(2,1)S(1)} %reshape.208), channel_id=1, replica_groups=mesh['dp'=8,'fsdp'=4] {'dp','fsdp'}, dimensions={0}, use_global_device_ids=true | all-gather | bytes 912384 | tf_op jit(solution)/shard_map/all_gather | solution.py:68
  147.8 7.3 reduce.5
  185.9 10.1 %reshape.215 = bf16[20,197,6,64]{3,2,1,0:T(8,128)(2,1)} reshape(bf16[3940,384]{1,0:T(8,128)(2,1)} %get-tuple-element.23) | data formatting | bytes 6051840 | tf_op jit(solution)/shard_map/reshape | solution.py:84
  196.0 9.7 %copy.50 = bf16[20,197,6,64]{1,3,2,0:T(8,128)(2,1)} copy(bf16[20,197,6,64]{3,2,1,0:T(8,128)(2,1)} %reshape.215) | data formatting | bytes 6051840 | tf_op jit(solution)/shard_map/reshape | solution.py:84
  205.7 10.1 %reshape.216 = bf16[20,197,6,64]{3,2,1,0:T(8,128)(2,1)} reshape(bf16[3940,384]{1,0:T(8,128)(2,1)} %slice.23) | data formatting | bytes 6051840 | tf_op jit(solution)/shard_map/reshape | solution.py:85
  215.8 10.2 %copy.51 = bf16[20,197,6,64]{1,3,2,0:T(8,128)(2,1)} copy(bf16[20,197,6,64]{3,2,1,0:T(8,128)(2,1)} %reshape.216) | data formatting | bytes 6051840 | tf_op jit(solution)/shard_map/reshape | solution.py:85
  233.2 9.8 %copy.52 = bf16[20,197,6,64]{1,3,2,0:T(8,128)(2,1)} copy(bf16[20,197,6,64]{3,2,1,0:T(8,128)(2,1)} %reshape.214) | data formatting | bytes 6051840 | tf_op jit(solution)/shard_map/reshape | solution.py:86
  243.0 14.9 %multiply_reduce_fusion.1 = (f32[20,6,197]{2,1,0:T(8,128)S(1)}, f32[20,6,197,197]{2,3,1,0:T(8,128)}) fusion(bf16[20,197,6,64]{1,3,2,0:T(8,128)(2,1)} %copy.50, bf16[20,197,6,64]{1,3,2,0:T(8,128)(2,1)} %copy.51), kind=kOutput, calls=%fused_computation.33 | convolution fusion | flops 605396736 | bytes 24774720 | tf_op jit(solution)/shard_map/ishd,ithd->ihst/dot_general | solution.py:88
  257.9 10.8 %fusion.16 = f32[20,6,197]{2,1,0:T(8,128)S(1)} fusion(f32[20,6,197,197]{2,3,1,0:T(8,128)} %get-tuple-element.36, f32[20,6,197]{2,1,0:T(8,128)S(1)} %get-tuple-element.35), kind=kLoop, calls=%fused_computation.32 | loop fusion | flops 13947600 | bytes 18817440 | tf_op jit(solution)/shard_map/reduce_sum | solution.py:93
  270.2 11.1 %convert_bitcast_fusion.1 = bf16[20,197,6,64]{1,3,2,0:T(8,128)(2,1)S(1)} fusion(bf16[20,197,6,64]{1,3,2,0:T(8,128)(2,1)S(1)} %copy-done.6, f32[20,6,197,197]{2,3,1,0:T(8,128)} %get-tuple-element.36, f32[20,6,197]{2,1,0:T(8,128)} %copy-done.21, f32[20,6,197]{2,1,0:T(8,128)} %copy-done.16), kind=kOutput, calls=%fused_computation.74 | convolution fusion | flops 616247552 | bytes 24869280 | tf_op jit(solution)/shard_map/ihst,ithd->ishd/dot_general | solution.py:96
  305.6 60.9 %fusion.2 = (bf16[3940,1536]{1,0:T(8,128)(2,1)}, f32[3940,1536]{1,0:T(8,128)}) fusion(f32[1536]{0:T(1024)S(1)} %split.45, bf16[384,1536]{1,0:T(8,128)(2,1)S(1)} %reshape.194, f32[3940,384]{1,0:T(8,128)} %copy-done.2, f32[384]{0:T(512)S(1)} %get-tuple-element.28, f32[384]{0:T(512)S(1)} %get-tuple-element.27, f32[3940]{0:T(1024)S(1)} %add_rsqrt_fusion.1, ...), kind=kOutput, calls=%fused_computation.9 | convolution fusion | flops 5054799360 | bytes 43583264 | tf_op jit(solution)/shard_map/dot_general | solution.py:101
  370.0 11.9 %add_add_fusion = f32[3940,384]{1,0:T(8,128)} fusion(f32[3940,384]{1,0:T(8,128)} %copy-done.2, bf16[3940,1536]{1,0:T(8,128)(2,1)} %get-tuple-element.39, bf16[1536,384]{1,0:T(8,128)(2,1)S(1)} %reshape.195, f32[384]{0:T(512)S(1)} %copy-done.33), kind=kOutput, calls=%fused_computation.62 | convolution fusion | flops 4650839040 | bytes 25388544 | tf_op jit(solution)/shard_map/dot_general | solution.py:103
  388.4 8.7 %convert_reduce_fusion.3 = (f32[384]{0:T(512)}, bf16[20,197,384]{2,1,0:T(8,128)(2,1)}, f32[20,197,384]{2,1,0:T(8,128)}, bf16[20,197,384]{2,1,0:T(8,128)(2,1)}) fusion(f32[20]{0:T(128)S(1)} %copy-done.36, bf16[20,197,384]{2,1,0:T(8,128)(2,1)S(1)} %copy-done.11, f32[20,197,384]{2,1,0:T(8,128)} %reshape.196), kind=kLoop, calls=%fused_computation.43 | loop fusion | flops 10590336 | bytes 21183056 | tf_op jit(solution)/shard_map/reduce_sum | solution.py:119
  401.5 18.0 %convert_reduce_fusion = (f32[1536]{0:T(1024)}, bf16[3940,1536]{1,0:T(8,128)(2,1)S(1)}) fusion(f32[3940,1536]{1,0:T(8,128)} %get-tuple-element.40, f32[1536]{0:T(1024)S(1)} %split.45, bf16[3940,384]{1,0:T(8,128)(2,1)} %convert_element_type.137, bf16[1536,384]{1,0:T(8,128)(2,1)S(1)} %copy-done.20), kind=kOutput, calls=%fused_computation.16 | convolution fusion | flops 4726485504 | bytes 40528896 | tf_op jit(solution)/shard_map/dot_general | solution.py:43
  426.6 10.9 %multiply_reduce_fusion.3 = (f32[384]{0:T(512)}, f32[3940]{0:T(1024)S(1)}, f32[3940]{0:T(1024)S(1)}, f32[384]{0:T(512)}, f32[3940,384]{1,0:T(8,128)}) fusion(f32[3940,384]{1,0:T(8,128)S(1)} %bitcast.50, f32[3940]{0:T(1024)S(1)} %add_rsqrt_fusion.1, f32[3940]{0:T(1024)S(1)} %broadcast_multiply_fusion.5, f32[384]{0:T(512)S(1)} %get-tuple-element.27, ...), kind=kOutput, calls=%fused_computation.53 | convolution fusion | flops 4661420544 | bytes 25454656 | tf_op jit(solution)/shard_map/dot_general | solution.py:43
  443.1 12.5 %fusion.28 = f32[1536,384]{1,0:T(8,128)} fusion(bf16[3940,1536]{1,0:T(8,128)(2,1)} %get-tuple-element.39, f32[3940,384]{1,0:T(8,128)} %reshape.197), kind=kOutput, calls=%fused_computation.76 | convolution fusion | flops 4649326080 | bytes 20514816 | tf_op jit(solution)/shard_map/dot_general | solution.py:37
  464.4 7.4 reshape.217
  471.8 9.7 %copy.56 = bf16[20,197,6,64]{1,3,2,0:T(8,128)(2,1)} copy(bf16[20,197,6,64]{3,2,1,0:T(8,128)(2,1)} %reshape.217) | data formatting | bytes 6051840 | tf_op jit(solution)/shard_map/reshape | solution.py:133
  481.5 13.9 %convert_reduce_fusion.1 = (f32[6,64]{1,0:T(8,128)S(1)}, bf16[20,197,6,64]{1,3,2,0:T(8,128)(2,1)}) fusion(bf16[20,197,6,64]{1,3,2,0:T(8,128)(2,1)} %copy.56, f32[20,6,197,197]{2,3,1,0:T(8,128)} %get-tuple-element.36, f32[20,6,197]{2,1,0:T(8,128)S(1)} %copy-done.9), kind=kOutput, calls=%fused_computation.39 | convolution fusion | flops 614616000 | bytes 24776256 | tf_op jit(solution)/shard_map/ihst,ishd->ithd/dot_general | solution.py:142
  495.4 22.3 %multiply_reduce_fusion = (f32[20,6,197]{2,1,0:T(8,128)S(1)}, f32[20,6,197,197]{2,3,1,0:T(8,128)}) fusion(f32[20,6,197,197]{2,3,1,0:T(8,128)} %get-tuple-element.36, f32[20,6,197]{2,1,0:T(8,128)S(1)} %copy-done.9, bf16[20,197,6,64]{1,3,2,0:T(8,128)(2,1)} %copy.56, bf16[20,197,6,64]{1,3,2,0:T(8,128)(2,1)} %copy.52), kind=kOutput, calls=%fused_computation.3 | convolution fusion | flops 614710912 | bytes 43497600 | tf_op jit(solution)/shard_map/ishd,ithd->ihst/dot_general | solution.py:139
  517.7 20.9 %multiply_convert_fusion = bf16[20,6,197,197]{2,3,1,0:T(8,128)(2,1)} fusion(f32[20,6,197,197]{2,3,1,0:T(8,128)} %get-tuple-element.43, f32[20,6,197,197]{2,3,1,0:T(8,128)} %get-tuple-element.36, f32[20,6,197]{2,1,0:T(8,128)S(1)} %get-tuple-element.42, f32[20,6,197]{2,1,0:T(8,128)S(1)} %copy-done.9), kind=kLoop, calls=%fused_computation.2 | loop fusion | flops 23285400 | bytes 46759920 | tf_op jit(solution)/shard_map/convert_element_type | solution.py:149
  538.6 14.1 %fusion.26 = bf16[20,197,6,64]{1,3,2,0:T(8,128)(2,1)} fusion(bf16[20,197,6,64]{1,3,2,0:T(8,128)(2,1)} %copy.50, bf16[20,6,197,197]{2,3,1,0:T(8,128)(2,1)} %multiply_convert_fusion), kind=kOutput, calls=%fused_computation.72 | convolution fusion | flops 599132160 | bytes 15366000 | tf_op jit(solution)/shard_map/ihst,ishd->ithd/dot_general | solution.py:155
  552.7 10.3 %convert_reduce_fusion.2 = (f32[6,64]{1,0:T(8,128)S(1)}, bf16[20,197,6,64]{1,3,2,0:T(8,128)(2,1)}) fusion(bf16[20,197,6,64]{1,3,2,0:T(8,128)(2,1)} %copy.51, bf16[20,6,197,197]{2,3,1,0:T(8,128)(2,1)} %multiply_convert_fusion), kind=kOutput, calls=%fused_computation.40 | convolution fusion | flops 602157696 | bytes 15367536 | tf_op jit(solution)/shard_map/ihst,ithd->ishd/dot_general | solution.py:151
  589.2 7.9 reshape.200
  603.7 8.0 reshape.199
  621.4 9.0 %fusion.27 = f32[384,1152]{1,0:T(8,128)S(1)} fusion(bf16[3940,1152]{0,1:T(8,128)(2,1)} %constant_dynamic-update-slice_fusion, f32[3940,384]{1,0:T(8,128)S(1)} %bitcast.48, f32[384]{0:T(512)S(1)} %copy-done.30, f32[3940]{0:T(1024)S(1)} %copy-done.22, f32[384]{0:T(512)S(1)} %copy-done.27, f32[3940]{0:T(1024)S(1)} %copy-done.23), kind=kOutput, calls=%fused_computation.75 | convolution fusion | flops 3493424640 | bytes 16933664 | tf_op jit(solution)/shard_map/dot_general | solution.py:37
  631.9 13.5 %multiply_reduce_fusion.4 = (f32[384]{0:T(512)S(1)}, f32[3940]{0:T(1024)S(1)}, f32[3940]{0:T(1024)S(1)}, f32[384]{0:T(512)S(1)}, f32[3940,384]{1,0:T(8,128)}) fusion(f32[3940,384]{1,0:T(8,128)} %reshape.188, f32[3940]{0:T(1024)S(1)} %copy-done.22, f32[3940]{0:T(1024)S(1)} %copy-done.23, f32[384]{0:T(512)S(1)} %copy-done.27, ...), kind=kOutput, calls=%fused_computation.55 | convolution fusion | flops 3499467776 | bytes 22133824 | tf_op jit(solution)/shard_map/dot_general | solution.py:43
  645.6 8.2 %add_convert_fusion.2 = bf16[3940,384]{1,0:T(8,128)(2,1)S(1)} fusion(f32[3940,384]{1,0:T(8,128)} %copy-done, f32[3940,384]{1,0:T(8,128)} %get-tuple-element.44, f32[3940,384]{1,0:T(8,128)} %reshape.188, f32[3940]{0:T(1024)S(1)} %broadcast_multiply_fusion.1, f32[3940]{0:T(1024)S(1)} %copy-done.22, f32[3940]{0:T(1024)S(1)} %broadcast_multiply_fusion.2, ...), kind=kLoop, calls=%fused_computation.57 | loop fusion | flops 13616640 | bytes 21246016 | tf_op jit(solution)/shard_map/convert_element_type | solution.py:173
  656.4 48.0 %all-reduce.5 = f32[4608]{0:T(1024)S(1)} all-reduce(f32[4608]{0:T(1024)S(1)} %constant_dynamic-update-slice_fusion.6), channel_id=6, replica_groups=mesh['dp'=8,'fsdp'=4] {'dp','fsdp'}, use_global_device_ids=true, to_apply=%region_24.0.clone | all-reduce | flops 4608 | bytes 36864
  705.0 99.6 %all-reduce.9.cloned.1.call-done = (f32[442368]{0:T(1024)}, f32[147456]{0:T(1024)}, f32[589824]{0:T(1024)}, f32[589824]{0:T(1024)}) async-done(((f32[442368]{0:T(1024)}, f32[147456]{0:T(1024)}, f32[589824]{0:T(1024)}, f32[589824]{0:T(1024)}), (f32[442368]{0:T(1024)}, f32[147456]{0:T(1024)}, f32[589824]{0:T(1024)}, f32[589824]{0:T(1024)})) %all-reduce.9.cloned.1.call-update) | async-done | bytes 7077904
  (168 shorter events, 171.2 us)
Async XLA Ops:
  7.2 49.1 %copy-start.3 = (bf16[20,197,384]{2,1,0:T(8,128)(2,1)S(1)}, bf16[20,197,384]{2,1,0:T(8,128)(2,1)}, u32[]{:S(2)}) copy-start(bf16[20,197,384]{2,1,0:T(8,128)(2,1)} %param.8) | copy-start | bytes 9077764
  7.2 295.7 %all-gather.5.cloned.1.call-start = ((), (), s32[]{:S(2)}) async-start(), calls=%async_computation | async-start | bytes 1216512 | tf_op jit(solution)/shard_map/all_gather | solution.py:70
  7.9 358.6 %all-gather.7.cloned.1.call-start = ((), (), s32[]{:S(2)}) async-start(), calls=%async_computation.1 | async-start | bytes 1216512 | tf_op jit(solution)/shard_map/all_gather | solution.py:71
  8.7 795.9 %all-reduce.9.cloned.1.call-start = ((), (), s32[]{:S(2)}) async-start(), calls=%async_computation.2 | async-start | bytes 14155776
  49.9 108.6 %copy-start.26 = (f32[384]{0:T(512)}, f32[384]{0:T(512)S(1)}, u32[]{:S(2)}) copy-start(f32[384]{0:T(512)S(1)} %get-tuple-element.32) | copy-start | bytes 4612
  49.9 108.6 %copy-start.29 = (f32[384]{0:T(512)}, f32[384]{0:T(512)S(1)}, u32[]{:S(2)}) copy-start(f32[384]{0:T(512)S(1)} %get-tuple-element.33) | copy-start | bytes 4612
  53.3 7.5 copy-start.28
  53.3 8.3 %copy-start.24 = (bf16[13824]{0:T(1024)(128)(2,1)S(1)}, bf16[13824]{0:T(1024)(128)(2,1)}, u32[]{:S(2)}) copy-start(bf16[13824]{0:T(1024)(128)(2,1)} %param.10) | copy-start | bytes 82948
  102.4 190.2 %copy-start.12 = (bf16[384,384]{1,0:T(8,128)(2,1)}, bf16[384,384]{1,0:T(8,128)(2,1)S(1)}, u32[]{:S(2)}) copy-start(bf16[384,384]{1,0:T(8,128)(2,1)S(1)} %reshape.193) | copy-start | bytes 884740
  170.6 6.2 copy-start.1
  257.9 10.9 %copy-start.16 = (f32[20,6,197]{2,1,0:T(8,128)}, f32[20,6,197]{2,1,0:T(8,128)S(1)}, u32[]{:S(2)}) copy-start(f32[20,6,197]{2,1,0:T(8,128)S(1)} %get-tuple-element.35) | copy-start | bytes 283684
  257.9 12.2 %copy-start.6 = (bf16[20,197,6,64]{1,3,2,0:T(8,128)(2,1)S(1)}, bf16[20,197,6,64]{1,3,2,0:T(8,128)(2,1)}, u32[]{:S(2)}) copy-start(bf16[20,197,6,64]{1,3,2,0:T(8,128)(2,1)} %copy.52) | copy-start | bytes 9077764
  292.6 6.4 copy-start.4
  305.6 60.9 %copy-start.17 = (bf16[384,1536]{1,0:T(8,128)(2,1)}, bf16[384,1536]{1,0:T(8,128)(2,1)S(1)}, u32[]{:S(2)}) copy-start(bf16[384,1536]{1,0:T(8,128)(2,1)S(1)} %reshape.194) | copy-start | bytes 3538948
  305.6 64.4 %copy-start.33 = (f32[384]{0:T(512)S(1)}, f32[384]{0:T(512)}, u32[]{:S(2)}) copy-start(f32[384]{0:T(512)} %get-tuple-element.26) | copy-start | bytes 4612
  382.0 6.4 copy-start.11
  382.0 6.4 copy-start.36
  397.2 22.4 %slice-start.2 = ((s8[6057984]{0:T(1024)(128)(4,1)}), s8[1863680]{0:T(1024)(128)(4,1)S(1)}, s32[]{:S(2)}) async-start(s8[6057984]{0:T(1024)(128)(4,1)} %bitcast.49), calls=%async_computation.5 | async-start | bytes 3727360
  401.5 18.0 %slice-start.3 = ((s8[6057984]{0:T(1024)(128)(4,1)}), s8[4194304]{0:T(1024)(128)(4,1)S(1)}, s32[]{:S(2)}) async-start(s8[6057984]{0:T(1024)(128)(4,1)} %bitcast.49), calls=%async_computation.6 | async-start | bytes 8388608
  419.6 7.0 copy-start.18
  437.5 18.2 %slice-start.4 = ((s8[6057984]{0:T(1024)(128)(4,1)}), s8[1863680]{0:T(1024)(128)(4,1)S(1)}, s32[]{:S(2)}) async-start(s8[6057984]{0:T(1024)(128)(4,1)} %bitcast.51), calls=%async_computation.7 | async-start | bytes 3727360
  443.1 12.5 %slice-start.5 = ((s8[6057984]{0:T(1024)(128)(4,1)}), s8[4194304]{0:T(1024)(128)(4,1)S(1)}, s32[]{:S(2)}) async-start(s8[6057984]{0:T(1024)(128)(4,1)} %bitcast.51), calls=%async_computation.8 | async-start | bytes 8388608
  443.1 12.5 %copy-start.7 = (f32[3940,384]{1,0:T(8,128)S(1)}, f32[3940,384]{1,0:T(8,128)}, u32[]{:S(2)}) copy-start(f32[3940,384]{1,0:T(8,128)} %reshape.197) | copy-start | bytes 18155524
  443.1 12.5 %copy-start.8 = (f32[3940,384]{1,0:T(8,128)S(1)}, f32[3940,384]{1,0:T(8,128)}, u32[]{:S(2)}) copy-start(f32[3940,384]{1,0:T(8,128)} %get-tuple-element.41) | copy-start | bytes 18155524
  471.8 9.7 %copy-start.9 = (f32[20,6,197]{2,1,0:T(8,128)S(1)}, f32[20,6,197]{2,1,0:T(8,128)}, u32[]{:S(2)}) copy-start(f32[20,6,197]{2,1,0:T(8,128)} %log_add_fusion) | copy-start | bytes 283684
  552.7 10.3 %copy-start.15 = (f32[384,1536]{1,0:T(8,128)S(1)}, f32[384,1536]{1,0:T(8,128)}, u32[]{:S(2)}) copy-start(f32[384,1536]{1,0:T(8,128)} %fusion.42) | copy-start | bytes 7077892
  552.7 11.9 %copy-start.14 = (f32[384,384]{1,0:T(8,128)S(1)}, f32[384,384]{1,0:T(8,128)}, u32[]{:S(2)}) copy-start(f32[384,384]{1,0:T(8,128)} %fusion.36) | copy-start | bytes 1769476
  611.7 9.7 %slice-start = ((s8[6057984]{0:T(1024)(128)(4,1)}), s8[4194304]{0:T(1024)(128)(4,1)S(1)}, s32[]{:S(2)}) async-start(s8[6057984]{0:T(1024)(128)(4,1)} %bitcast.47), calls=%async_computation.3 | async-start | bytes 8388608
  615.6 5.8 copy-start.22
  615.6 5.8 copy-start.23
  615.6 5.8 copy-start.27
  615.6 5.8 copy-start.30
  (14 other events, 37.5 us)
Sparse Core Ops, SparseCore 0:
  10.9 54.7 all-gather.4
  68.6 54.9 all-gather.6
  631.9 172.6 all-reduce.8
where the time goes:
time: 830 us; the launch traced here: 817 us
  matrix products  248 us (30%)
  local copies, waits for them, and re-layouts  203 us (24%)
  blocking collectives  169 us (20%)
  waiting for transfers between devices  101 us (12%)
  other arithmetic  80.8 us (10%)
  between operations  15.2 us (2%)
    unnamed x4, waiting for transfers between devices  101 us
    unnamed x2, blocking collectives  87.7 us
    dot_general x1, matrix products, body(): jnp.dot(second_in, wup, preferred_element_type=jnp.float32) + bias_up  60.9 us
    all_gather x1, blocking collectives, body(): lax.all_gather(shards[0], ('dp', 'fsdp'), axis=0, tiled=True)  45.4 us
    dot_general x4, matrix products, times_trans(): lax.dot_general(left, right, (((1,), (1,)), ((), ())), preferred_element_...  44.8 us
    all_gather x1, blocking collectives, body(): lax.all_gather(shards[1], ('dp', 'fsdp'), axis=0, tiled=True)  36.1 us
    dot_general x4, matrix products, over_rows(): lax.dot_general(left, right, (((0,), (0,)), ((), ())), preferred_element_...  31.2 us
    unnamed x105, local copies, waits for them, and re-layouts  26 us
  transfers between devices with their start and end apart: 3, of which 1 were waited for; matrix products, arithmetic and copies ran while one was open for 31% of the time, Pallas kernels for 0%

commit v1 on v0

v1 whole, which is shorter than its diff:
```python
import math

import jax
import jax.numpy as jnp
from jax import lax
from jax.experimental import pallas as pl
from jax.experimental.pallas import tpu as pltpu
from jax.sharding import PartitionSpec as P

HEADS = 6
HEAD_DIM = 64
EPS = 1e-06
F32 = jnp.float32
BF16 = jnp.bfloat16


def mm(a, b):
    return lax.dot_general(a, b, (((1,), (0,)), ((), ())), preferred_element_type=F32)


def mm_t(a, b):
    return lax.dot_general(a, b, (((1,), (1,)), ((), ())), preferred_element_type=F32)


def t_mm(a, b):
    return lax.dot_general(a, b, (((0,), (0,)), ((), ())), preferred_element_type=F32)


def norm_parts(values, width):
    mean = jnp.sum(values, axis=-1, keepdims=True) * (1.0 / width)
    center = values - mean
    var = jnp.sum(center * center, axis=-1, keepdims=True) * (1.0 / width)
    inverse = lax.rsqrt(var + EPS)
    return center * inverse, inverse


def norm_back(upstream, normed, inverse, gain, width):
    scaled = upstream * gain
    m1 = jnp.sum(scaled, axis=-1, keepdims=True) * (1.0 / width)
    m2 = jnp.sum(scaled * normed, axis=-1, keepdims=True) * (1.0 / width)
    return inverse * (scaled - m1 - normed * m2)


def gelu_both(z):
    ez = jnp.exp(-0.5 * z * z)
    t = 1.0 / (1.0 + (0.3275911 * 0.7071067811865476) * jnp.abs(z))
    poly = ((((1.061405429 * t - 1.453152027) * t + 1.421413741) * t - 0.284496736) * t + 0.254829592) * t
    half = 0.5 * poly * ez
    cumul = jnp.where(z >= 0.0, 1.0 - half, half)
    return z * cumul, cumul + z * (ez * 0.3989422804014327)


def layer_kernel(
    count_ref, x_ref, ct_ref, wqkv_ref, wout_ref, wup_ref, wdown_ref, small_ref, bup_ref,
    out_ref, gx_ref, gqkv_ref, gout_ref, gup_ref, gdown_ref, gsmall_ref, gbup_ref,
    xs, cs, n1s, qs, ks, vs, pbs, os_, y1s, n2s, a1s, a2s, acts, dzs, dos, dqkvs,
):
    step = pl.program_id(0)
    seq, width = x_ref.shape[1], x_ref.shape[2]
    rows = xs.shape[0]
    hidden = wup_ref.shape[1]
    scale = 1.0 / math.sqrt(HEAD_DIM)

    @pl.when(step == 0)
    def _():
        xs[...] = jnp.zeros_like(xs)
        cs[...] = jnp.zeros_like(cs)
        for ref in (gqkv_ref, gout_ref, gup_ref, gdown_ref, gsmall_ref, gbup_ref):
            ref[...] = jnp.zeros_like(ref)

    live = step < count_ref[0]

    @pl.when(jnp.logical_not(live))
    def _():
        out_ref[...] = jnp.zeros_like(out_ref)
        gx_ref[...] = jnp.zeros_like(gx_ref)

    @pl.when(live)
    def _():
        xs[0:seq, :] = x_ref[0]
        cs[0:seq, :] = ct_ref[0]
        g1, c1 = small_ref[0:1, :], small_ref[1:2, :]
        bq, bv, bo = small_ref[2:3, :], small_ref[3:4, :], small_ref[4:5, :]
        g2, c2, b2 = small_ref[5:6, :], small_ref[6:7, :], small_ref[7:8, :]
        n1, inv1 = norm_parts(xs[...].astype(F32), width)
        n1s[...] = n1
        a1s[...] = (n1 * g1 + c1).astype(BF16)
        qs[...] = (mm(a1s[...], wqkv_ref[:, :width]) + bq).astype(BF16)
        ks[...] = mm(a1s[...], wqkv_ref[:, width : 2 * width]).astype(BF16)
        vs[...] = (mm(a1s[...], wqkv_ref[:, 2 * width :]) + bv).astype(BF16)
        lane = lax.broadcasted_iota(jnp.int32, (rows, 2 * HEAD_DIM), 1)
        halves = (lane < HEAD_DIM, lane >= HEAD_DIM)
        keyrow = lax.broadcasted_iota(jnp.int32, (rows, rows), 0)
        zero = jnp.zeros((rows, 2 * HEAD_DIM), BF16)
        for pair in range(HEADS // 2):
            cols = slice(pair * 2 * HEAD_DIM, (pair + 1) * 2 * HEAD_DIM)
            qp, kp, vp = qs[:, cols], ks[:, cols], vs[:, cols]
            both = None
            for h in range(2):
                km = jnp.where(halves[h], kp, zero)
                vm = jnp.where(halves[h], vp, zero)
                scores = mm_t(km, qp) * scale
                scores = jnp.where(keyrow < seq, scores, -1e30)
                top = jnp.max(scores, axis=0, keepdims=True)
                expo = jnp.exp(scores - top)
                total = jnp.sum(expo, axis=0, keepdims=True)
                prob = expo * (1.0 / total)
                pbs[pair * 2 + h] = prob.astype(BF16)
                part = t_mm(pbs[pair * 2 + h], vm)
                both = part if both is None else both + part
            os_[:, cols] = both.astype(BF16)
        y1 = xs[...].astype(F32) + (mm(os_[...], wout_ref[...]) + bo)
        y1s[...] = y1
        n2, inv2 = norm_parts(y1, width)
        n2s[...] = n2
        a2s[...] = (n2 * g2 + c2).astype(BF16)
        tile = 256
        for j in range(hidden // tile):
            cols = slice(j * tile, (j + 1) * tile)
            z = mm(a2s[...], wup_ref[:, cols]) + bup_ref[:, cols]
            act, slope = gelu_both(z)
            acts[:, cols] = act.astype(BF16)
            dz = (mm_t(cs[...], wdown_ref[cols, :]) * slope).astype(BF16)
            dzs[:, cols] = dz
            gbup_ref[:, cols] += jnp.sum(dz.astype(F32), axis=0, keepdims=True)
        y = y1s[...] + mm(acts[...], wdown_ref[...]) + b2
        out_ref[0] = y[:seq].astype(BF16)
        gdown_ref[...] += t_mm(acts[...], cs[...])
        gup_ref[...] += t_mm(a2s[...], dzs[...])
        da2 = mm_t(dzs[...], wup_ref[...])
        ct = cs[...].astype(F32)
        n2 = n2s[...]
        gsmall_ref[7:8, :] += jnp.sum(ct, axis=0, keepdims=True)
        gsmall_ref[5:6, :] += jnp.sum(da2 * n2, axis=0, keepdims=True)
        gsmall_ref[6:7, :] += jnp.sum(da2, axis=0, keepdims=True)
        dy1 = ct + norm_back(da2, n2, inv2, g2, width)
        y1s[...] = dy1
        da = dy1.astype(BF16)
        gsmall_ref[4:5, :] += jnp.sum(da.astype(F32), axis=0, keepdims=True)
        gout_ref[...] += t_mm(os_[...], da)
        dos[...] = mm_t(da, wout_ref[...]).astype(BF16)
        for pair in range(HEADS // 2):
            cols = slice(pair * 2 * HEAD_DIM, (pair + 1) * 2 * HEAD_DIM)
            qp, kp, vp, dop = qs[:, cols], ks[:, cols], vs[:, cols], dos[:, cols]
            dq = dk = dv = None
            for h in range(2):
                qm = jnp.where(halves[h], qp, zero)
                km = jnp.where(halves[h], kp, zero)
                vm = jnp.where(halves[h], vp, zero)
                dom = jnp.where(halves[h], dop, zero)
                pb = pbs[pair * 2 + h]
                prob = pb.astype(F32)
                dp = mm_t(vm, dop)
                inner = jnp.sum(prob * dp, axis=0, keepdims=True)
                ds = (prob * (dp - inner)).astype(BF16)
                dv_h = mm(pb, dom)
                dk_h = mm(ds, qm)
                dq_h = t_mm(ds, km)
                dq = dq_h if dq is None else dq + dq_h
                dk = dk_h if dk is None else dk + dk_h
                dv = dv_h if dv is None else dv + dv_h
            base = pair * 2 * HEAD_DIM
            dqkvs[:, base : base + 2 * HEAD_DIM] = (dq * scale).astype(BF16)
            dqkvs[:, width + base : width + base + 2 * HEAD_DIM] = (dk * scale).astype(BF16)
            dqkvs[:, 2 * width + base : 2 * width + base + 2 * HEAD_DIM] = dv.astype(BF16)
        gsmall_ref[2:3, :] += jnp.sum(dqkvs[:, :width].astype(F32), axis=0, keepdims=True)
        gsmall_ref[3:4, :] += jnp.sum(dqkvs[:, 2 * width :].astype(F32), axis=0, keepdims=True)
        gqkv_ref[...] += t_mm(a1s[...], dqkvs[...])
        da1 = mm_t(dqkvs[...], wqkv_ref[...])
        n1 = n1s[...]
        gsmall_ref[0:1, :] += jnp.sum(da1 * n1, axis=0, keepdims=True)
        gsmall_ref[1:2, :] += jnp.sum(da1, axis=0, keepdims=True)
        gx = y1s[...] + norm_back(da1, n1, inv1, g1, width)
        gx_ref[0] = gx[:seq].astype(BF16)


def run_layer(count, tokens, cotangent, wqkv, wout, wup, wdown, small, bup):
    slots, seq, width = tokens.shape
    hidden = wup.shape[1]
    rows = (seq + 15) // 16 * 16

    def whole(shape):
        return pl.BlockSpec(shape, lambda i, c: (0,) * len(shape), pipeline_mode=pl.Buffered(1))

    def image():
        return pl.BlockSpec((1, seq, width), lambda i, c: (i, 0, 0))

    return pl.pallas_call(
        layer_kernel,
        grid_spec=pltpu.PrefetchScalarGridSpec(
            num_scalar_prefetch=1,
            grid=(slots,),
            in_specs=[
                image(), image(),
                whole((width, 3 * width)), whole((width, width)), whole((width, hidden)),
                whole((hidden, width)), whole((8, width)), whole((1, hidden)),
            ],
            out_specs=[
                image(), image(),
                whole((width, 3 * width)), whole((width, width)), whole((width, hidden)),
                whole((hidden, width)), whole((8, width)), whole((1, hidden)),
            ],
            scratch_shapes=[
                pltpu.VMEM((rows, width), BF16),
                pltpu.VMEM((rows, width), BF16),
                pltpu.VMEM((rows, width), F32),
                pltpu.VMEM((rows, width), BF16),
                pltpu.VMEM((rows, width), BF16),
                pltpu.VMEM((rows, width), BF16),
                pltpu.VMEM((HEADS, rows, rows), BF16),
                pltpu.VMEM((rows, width), BF16),
                pltpu.VMEM((rows, width), F32),
                pltpu.VMEM((rows, width), F32),
                pltpu.VMEM((rows, width), BF16),
                pltpu.VMEM((rows, width), BF16),
                pltpu.VMEM((rows, hidden), BF16),
                pltpu.VMEM((rows, hidden), BF16),
                pltpu.VMEM((rows, width), BF16),
                pltpu.VMEM((rows, 3 * width), BF16),
            ],
        ),
        out_shape=[
            jax.ShapeDtypeStruct(tokens.shape, BF16),
            jax.ShapeDtypeStruct(tokens.shape, BF16),
            jax.ShapeDtypeStruct((width, 3 * width), F32),
            jax.ShapeDtypeStruct((width, width), F32),
            jax.ShapeDtypeStruct((width, hidden), F32),
            jax.ShapeDtypeStruct((hidden, width), F32),
            jax.ShapeDtypeStruct((8, width), F32),
            jax.ShapeDtypeStruct((1, hidden), F32),
        ],
        compiler_params=pltpu.CompilerParams(
            dimension_semantics=("arbitrary",), vmem_limit_bytes=48 * 1024 * 1024
        ),
    )(count, tokens, cotangent, wqkv, wout, wup, wdown, small, bup)


def body(tokens, image_count, w_qkv, w_out, w_fc1, w_fc2, norm_bias, cotangent):
    slots, seq, width = tokens.shape
    shards = (w_qkv, w_out, w_fc1, w_fc2, norm_bias)
    sizes = [s.shape[0] for s in shards]
    cuts = [sum(sizes[: i + 1]) for i in range(len(sizes) - 1)]
    gathered = lax.all_gather(jnp.concatenate(shards), ("dp", "fsdp"), axis=0, tiled=False)
    parts = [p.reshape(-1) for p in jnp.split(gathered, cuts, axis=1)]
    hidden = parts[2].shape[0] // width
    wqkv = parts[0].reshape(width, 3 * width)
    wout = parts[1].reshape(width, width)
    wup = parts[2].reshape(width, hidden)
    wdown = parts[3].reshape(hidden, width)
    vec = parts[4].astype(F32)
    small = jnp.concatenate([vec[: 7 * width], vec[7 * width + hidden :]]).reshape(8, width)
    bup = vec[7 * width : 7 * width + hidden].reshape(1, hidden)
    output, grad_tokens, gqkv, gout, gup, gdown, gsmall, gbup = run_layer(
        image_count, tokens, cotangent, wqkv, wout, wup, wdown, small, bup
    )
    flat = gsmall.reshape(-1)
    gvec = jnp.concatenate([flat[: 7 * width], gbup.reshape(-1), flat[7 * width :]])
    devices = gathered.shape[0]
    terms = jnp.concatenate(
        [g.reshape(devices, -1) for g in (gqkv, gout, gup, gdown, gvec)], axis=1
    ).reshape(-1)
    summed = lax.psum_scatter(terms, ("dp", "fsdp"), scatter_dimension=0, tiled=True)
    return (output, grad_tokens, *jnp.split(summed, cuts))


def solution(mesh):
    both = P(("dp", "fsdp"))
    images = P(("dp", "fsdp"), None, None)
    return jax.shard_map(
        body,
        mesh=mesh,
        in_specs=(images, both, both, both, both, both, both, images),
        out_specs=(images, images, both, both, both, both, both),
        check_vma=False,
    )
```

time: 830 us -> 539 us (0.65); the launches traced: 817 us -> 535 us
  waiting for transfers between devices: 101 us -> 397 us
  matrix products: 248 us -> 0 us
  blocking collectives: 169 us -> 0 us
  local copies, waits for them, and re-layouts: 203 us -> 66.1 us
  other arithmetic: 80.8 us -> 1.26 us
  Pallas kernels: 0 us -> 56.7 us
    unnamed x4, waiting for transfers between devices: 101 us -> 397 us
    dot_general x18 -> x0, matrix products: 248 us -> none  [the longest x1 60.9 us: body(): jnp.dot(second_in, wup, preferred_element_type=jnp.float32) + bias_up]
    reshape x22 -> x8, local copies, waits for them, and re-layouts: 129 us -> 19.6 us  [the longest x1 10.6 us: body(): terms = jnp.concatenate([g.reshape(devices, -1) for g in (gqkv, gout, gup...]
    unnamed x2 -> x0, blocking collectives: 87.7 us -> none
    all_gather x2 -> x0, blocking collectives: 81.5 us -> none  [the longest x1 45.4 us: body(): lax.all_gather(shards[0], ('dp', 'fsdp'), axis=0, tiled=True)]
    pallas_call x0 -> x1, Pallas kernels: none -> 56.7 us  [run_layer(): pl.pallas_call(layer_kernel, grid_spec=pltpu.PrefetchScalarGridSpec(num_s...]
    convert_element_type x8 -> x1, local copies, waits for them, and re-layouts: 41.2 us -> 0.84 us  [body(): vec = parts[4].astype(F32)]
    convert_element_type x5 -> x1, other arithmetic: 39.2 us -> 0.62 us  [body(): vec = parts[4].astype(F32)]
  transfers between devices with their start and end apart: 3 -> 2, of which waited for: 1 -> 2; matrix products, arithmetic and copies ran while one was open for 31% -> 0% of each run, Pallas kernels for 0% -> 0%
where the time goes in v1:
time: 539 us; the launch traced here: 535 us
  waiting for transfers between devices  397 us (74%)
  local copies, waits for them, and re-layouts  66.1 us (12%)
  Pallas kernels  56.7 us (11%)
  between operations  14.9 us (3%)
    unnamed x4, waiting for transfers between devices  397 us
    pallas_call x1, Pallas kernels, run_layer(): pl.pallas_call(layer_kernel, grid_spec=pltpu.PrefetchScalarGridSpec(num_s...  56.7 us
    unnamed x30, local copies, waits for them, and re-layouts  19.5 us
  transfers between devices with their start and end apart: 2, of which 2 were waited for; matrix products, arithmetic and copies ran while one was open for 0% of the time, Pallas kernels for 0%

profile of v1, /device:TPU:11, one launch (start us, length us, event | category | flops | bytes accessed | tf_op | source)
XLA Modules:
  0.0 535.5 jit_solution(12720902148792197944)
XLA Ops:
  7.2 1.1 dynamic-update-slice.6
  8.4 1.0 dynamic-update-slice.7
  9.3 0.8 constant_dynamic-update-slice_fusion.7
  10.1 0.8 constant_dynamic-update-slice_fusion.6
  12.5 2.2 dynamic-update-slice
  14.7 1.8 copy-done.7
  17.2 137.9 %all-reduce.5.cloned.1.call-done = bf16[1774080]{0:T(1024)(128)(2,1)} async-done(((bf16[1774080]{0:T(1024)(128)(2,1)}), bf16[1774080]{0:T(1024)(128)(2,1)}) %all-reduce.5.cloned.1.call-update) | async-done | bytes 3548176
  155.1 6.6 %reshape.57 = bf16[32,55440]{1,0:T(8,128)(2,1)S(1)} reshape(bf16[1774080]{0:T(1024)(128)(2,1)} %all-reduce.5.cloned.1.call-done) | data formatting | bytes 7096320 | tf_op jit(solution)/shard_map/all_gather | solution.py:243
  161.7 1.0 split.40
  162.7 0.8 split.41
  163.4 1.6 fusion.1
  165.6 0.8 reshape.56
  167.7 2.5 reshape_reshape.12.wqkv_ref
  170.2 1.3 reshape_reshape.13.wout_ref
  171.5 2.9 reshape_reshape.14.wup_ref
  174.4 1.6 reshape_reshape.15.wdown_ref
  178.1 56.7 %shard_map.135 = (bf16[20,197,384]{2,1,0:T(8,128)(2,1)}, bf16[20,197,384]{2,1,0:T(8,128)(2,1)}, f32[384,1152]{1,0:T(8,128)S(1)}, f32[384,384]{1,0:T(8,128)S(1)},...) custom-call(s32[1]{0:T(128)S(6)} %copy.27.count_ref, ...), custom_call_target="tpu_custom_call" | custom-call | tf_op jit(solution)/shard_map/pallas_call | solution.py:188
  234.8 1.2 copy-done
  236.0 0.8 copy-done.1
  238.0 1.8 reshape.49
  239.8 1.3 constant_dynamic-update-slice_fusion.4
  241.3 3.5 reshape.51
  244.7 2.1 reshape.52
  247.0 0.9 constant_dynamic-update-slice_fusion.3
  247.9 3.3 constant_dynamic-update-slice_fusion.2
  251.1 1.6 constant_dynamic-update-slice_fusion.1
  253.4 10.6 %reshape.55 = f32[1774080]{0:T(1024)} reshape(f32[32,55440]{1,0:T(8,128)} %constant_dynamic-update-slice_fusion) | data formatting | bytes 14192640 | tf_op jit(solution)/shard_map/reshape | solution.py:261
  264.1 258.6 %all-reduce.7.cloned.1.call-done = f32[1774080]{0:T(1024)} async-done(((f32[1774080]{0:T(1024)}), f32[1774080]{0:T(1024)}) %all-reduce.7.cloned.1.call-update) | async-done | bytes 7096336
  522.6 1.5 dynamic-slice.1
  524.2 1.4 dynamic-slice.2
  525.6 1.3 dynamic-slice.5
  526.9 1.7 fusion
  (39 shorter events, 7.6 us)
Async XLA Ops:
  7.2 147.9 %all-reduce.5.cloned.1.call-start = ((), (), s32[]{:S(2)}) async-start(), calls=%async_computation | async-start | bytes 7098368
  11.6 0.6 copy-start.8
  14.7 1.8 copy-start.7
  16.5 506.2 %all-reduce.7.cloned.1.call-start = ((), (), s32[]{:S(2)}) async-start(), calls=%async_computation.1 | async-start | bytes 14196736
  166.5 0.6 copy-start.9
  167.7 8.4 %slice-start = ((f32[4608]{0:T(1024)}), f32[2688]{0:T(1024)S(1)}, s32[]{:S(2)}) async-start(f32[4608]{0:T(1024)} %copy-done.9), calls=%async_computation.2 | async-start | bytes 24576 | tf_op jit(solution)/shard_map/slice | solution.py:251
  234.7 1.2 copy-start
  236.0 0.8 copy-start.1
  236.8 0.6 copy-start.3
  237.4 0.6 copy-start.5
  238.0 3.2 copy-start.2
  241.3 5.5 %copy-start.4 = (f32[8,384]{1,0:T(8,128)S(1)}, f32[8,384]{1,0:T(8,128)}, u32[]{:S(2)}) copy-start(f32[8,384]{1,0:T(8,128)} %copy-done.3) | copy-start | bytes 36868
  244.7 2.1 copy-start.6
Sparse Core Ops, SparseCore 0:
  16.6 138.4 all-reduce.4
  264.2 258.4 all-reduce.6
